TPU v7x, 128 devices: a whole 4x4x4 slice. The times are simulated.
128 devices in a mesh: tx: 8 (over x, core), ty: 16 (over z, y).
Axes of the slice: x: 4, y: 4, z: 4, core: 2. Of those that a mesh axis runs over, the one named last changes fastest.
Arguments:
- solution: float32 [4, 1024, 4096], P(None, 'tx', 'ty'), may hold values from -6 to 6
- residual: float32 [4, 1024, 4096], P(None, 'tx', 'ty')
- direction: float32 [4, 1024, 4096], P(None, 'tx', 'ty')
- blocks: bfloat16 [32768, 128, 256], P(('tx', 'ty')), may hold values from -0.375 to 0.375
- bin_owner: int32 [32768, 1], P(('tx', 'ty')), may hold values from 0 to 127; in each aligned block of 256 rows (0 to 255, 256 to 511, ...) at most 3 rows name the same one
- bin_tile: int32 [32768], P(('tx', 'ty')), may hold values from 0 to 127
Outputs:
- next_solution: float32 [4, 1024, 4096], P(None, 'tx', 'ty')
- next_residual: float32 [4, 1024, 4096], P(None, 'tx', 'ty')
- next_direction: float32 [4, 1024, 4096], P(None, 'tx', 'ty')
Inputs may be any that keep to these rules, and one draw needn't show every extreme that they name: `bin_owner`: among the bins of one device, at most 3 name the same owner, and on some devices some owner is named by exactly 3 of them.
All inputs are finite; a program needn't handle non-finite values.
Results may differ from a plain program's by a relative error of at most 0.0024.
Values may be sent and summed in bfloat16 or wider, within the bound.
A program may use at most 128 MiB of HBM per device.

v0:
```python
import jax
import jax.numpy as jnp
from jax import lax
from jax.sharding import PartitionSpec as P

TILE_SIDE = 16
smooth_weight = 0.25


def padded_2(shard, sides, width):
    for axis, dim in sides:
        size, length = (lax.axis_size(axis), shard.shape[dim])
        up = [(i, (i + 1) % size) for i in range(size - 1)]
        down = [(j, i) for i, j in up]
        last = lax.slice_in_dim(shard, length - width, length, axis=dim)
        initial = lax.slice_in_dim(shard, 0, width, axis=dim)
        before = lax.ppermute(last, axis, up)
        after = lax.ppermute(initial, axis, down)
        shard = jnp.concatenate([before, shard, after], axis=dim)
    return shard


def to_tiles(field):
    beacons, rows, cols = field.shape
    across = rows // TILE_SIDE
    down = cols // TILE_SIDE
    shaped = field.reshape(beacons, across, TILE_SIDE, down, TILE_SIDE).transpose(1, 3, 0, 2, 4)
    return shaped.reshape(across * down, beacons, TILE_SIDE * TILE_SIDE)


def to_field(tiles, rows, cols):
    beacons = tiles.shape[1]
    across = rows // TILE_SIDE
    down = cols // TILE_SIDE
    shaped = tiles.reshape(across, down, beacons, TILE_SIDE, TILE_SIDE).transpose(2, 0, 3, 1, 4)
    return shaped.reshape(beacons, rows, cols)


def laplace_local(field):
    padded = padded_2(field.astype(jnp.bfloat16), (("tx", 1), ("ty", 2)), 1).astype(field.dtype)
    near = padded[:, 2:, 1:-1] + padded[:, :-2, 1:-1] + padded[:, 1:-1, 2:] + padded[:, 1:-1, :-2]
    return 4.0 * field - near


def per_device(solution, residual, direction, blocks, bin_owner, bin_tile):
    beacons, rows, cols = direction.shape
    cells = TILE_SIDE * TILE_SIDE
    across_x = lax.axis_size("tx")
    across_y = lax.axis_size("ty")
    devices = across_x * across_y
    count = blocks.shape[0]
    cap = max(2, 3 * count // (2 * devices))
    owner = bin_owner[:, 0]
    member = (owner[:, None] == jnp.arange(devices, dtype=jnp.int32)[None, :]).astype(jnp.int32)
    before = jnp.cumsum(member, axis=0) - member
    rank = jnp.sum(before * member, axis=1)
    slot = owner * cap + rank
    request = jnp.full((devices * cap,), -1, jnp.int32).at[slot].set(bin_tile)
    wanted = lax.all_to_all(
        request.reshape(devices, cap), ("tx", "ty"), split_axis=0, concat_axis=0, tiled=True
    )
    wanted = jnp.maximum(wanted.reshape(devices * cap), 0)
    own_tiles = to_tiles(direction.astype(jnp.bfloat16))
    outgoing = jnp.take(own_tiles, wanted, axis=0)
    fetched = lax.all_to_all(
        outgoing.reshape(devices, cap, beacons, cells),
        ("tx", "ty"),
        split_axis=0,
        concat_axis=0,
        tiled=True,
    )
    fetched = fetched.reshape(devices * cap, beacons, cells)
    picked = jnp.take(fetched, slot, axis=0)
    samples = jnp.einsum("bsc,bkc->bks", blocks, picked, preferred_element_type=jnp.float32).astype(
        jnp.bfloat16
    )
    adjoint = jnp.einsum("bsc,bks->bkc", blocks, samples, preferred_element_type=jnp.float32)
    returned = jnp.zeros((devices * cap, beacons, cells), jnp.float32).at[slot].set(adjoint)
    arrived = lax.all_to_all(
        returned.reshape(devices, cap, beacons, cells),
        ("tx", "ty"),
        split_axis=0,
        concat_axis=0,
        tiled=True,
    )
    arrived = arrived.reshape(devices * cap, beacons, cells)
    data_tiles = jnp.zeros(own_tiles.shape, jnp.float32).at[wanted].add(arrived)
    image = to_field(data_tiles, rows, cols) + smooth_weight * laplace_local(direction)
    norm_old = lax.psum(jnp.sum(residual * residual, axis=(1, 2)), ("tx", "ty"))
    curvature = lax.psum(jnp.sum(direction * image, axis=(1, 2)), ("tx", "ty"))
    alpha = norm_old / curvature
    next_residual = residual - alpha[:, None, None] * image
    norm_new = lax.psum(jnp.sum(next_residual * next_residual, axis=(1, 2)), ("tx", "ty"))
    next_solution = solution + alpha[:, None, None] * direction
    next_direction = next_residual + (norm_new / norm_old)[:, None, None] * direction
    return (next_solution, next_residual, next_direction)


def solution(mesh):
    placed = (
        P(None, "tx", "ty"),
        P(None, "tx", "ty"),
        P(None, "tx", "ty"),
        P(("tx", "ty"), None, None),
        P(("tx", "ty"), None),
        P(("tx", "ty")),
    )
    return jax.shard_map(
        per_device,
        mesh=mesh,
        in_specs=placed,
        out_specs=(P(None, "tx", "ty"), P(None, "tx", "ty"), P(None, "tx", "ty")),
        check_vma=False,
    )
```

profile of v0, /device:TPU:1, one launch (start us, length us, event | category | flops | bytes accessed | tf_op | source)
XLA Modules:
  0.0 294.0 jit_solution(3272720926653905522)
XLA Ops:
  0.6 0.8 copy.23
  1.4 0.2 fusion.10
  1.7 0.9 fusion.12
  2.6 0.7 and_reduce_fusion
  3.3 1.6 scatter_custom_fusion
  4.8 0.8 all_to_all.12
  5.7 11.5 %all-to-all-start = ((s32[128,1,3]{2,1,0:T(1,128)}), s32[128,1,3]{2,1,0:T(1,128)S(1)}, u32[]{:S(2)}, u32[]{:S(2)}) async-start(s32[128,1,3]{2,1,0:T(1,128)} %bitcast.7), calls=%async_computation | async-start | bytes 131072 | tf_op jit(solution)/shard_map/all_to_all | solution.py:59
  17.2 1.1 convert_element_type.19
  18.3 2.5 reshape.85
  20.7 2.1 copy.33
  22.9 2.0 reshape.86
  24.9 0.2 copy.29
  25.1 1.8 all-to-all-done
  26.9 0.2 maximum_reduce_fusion
  27.1 0.2 reshape.126
  27.3 0.1 maximum_compare_fusion
  27.4 0.1 copy.26
  27.5 0.1 copy.27
  27.7 2.3 gather_fusion
  30.0 1.4 broadcast_select_fusion
  31.4 8.0 %all-to-all-start.1 = ((bf16[128,3,4,256]{3,2,1,0:T(4,128)(2,1)}), bf16[128,3,4,256]{3,2,1,0:T(4,128)(2,1)S(1)}, u32[]{:S(2)}, u32[]{:S(2)}) async-start(bf16[128,3,4,256]{3,2,1,0:T(4,128)(2,1)} %broadcast_select_fusion), calls=%async_computation.1 | async-start | bytes 1572864 | tf_op jit(solution)/shard_map/all_to_all | solution.py:65
  39.5 16.6 %all-to-all-done.1 = bf16[128,3,4,256]{3,2,1,0:T(4,128)(2,1)S(1)} async-done(((bf16[128,3,4,256]{3,2,1,0:T(4,128)(2,1)}), bf16[128,3,4,256]{3,2,1,0:T(4,128)(2,1)S(1)}, u32[]{:S(2)}, u32[]{:S(2)}) %all-to-all-start.1) | async-done | bytes 786464 | tf_op jit(solution)/shard_map/all_to_all | solution.py:65
  56.1 1.2 gather_fusion.1
  57.3 16.9 %fusion = f32[256,4,256]{2,1,0:T(4,128)S(1)} fusion(bf16[256,128,256]{2,1,0:T(8,128)(2,1)} %param.9, bf16[256,4,256]{2,1,0:T(4,128)(2,1)S(1)} %gather_fusion.1, pred[256]{0:T(512)(128)(4,1)S(1)} %get-tuple-element.9), kind=kOutput, calls=%fused_computation.8 | convolution fusion | flops 134610944 | bytes 18350336 | tf_op jit(solution)/shard_map/bsc,bks->bkc/dot_general | solution.py:77
  74.1 1.4 broadcast_in_dim.38
  75.5 23.9 %scatter_fusion = f32[384,4,256]{2,1,0:T(4,128)} fusion(f32[384,4,256]{2,1,0:T(4,128)} %broadcast_in_dim.38, s32[256]{0:T(256)S(1)} %bitcast.49, f32[256,4,256]{2,1,0:T(4,128)S(1)} %fusion), kind=kCustom, calls=%fused_computation.3 | custom fusion | bytes 3146752 | tf_op jit(solution)/shard_map/scatter | solution.py:78
  99.4 4.2 %all-to-all-start.2 = ((f32[128,3,4,256]{3,2,1,0:T(4,128)}), f32[128,3,4,256]{3,2,1,0:T(4,128)S(1)}, u32[]{:S(2)}, u32[]{:S(2)}) async-start(f32[128,3,4,256]{3,2,1,0:T(4,128)} %bitcast.12), calls=%async_computation.2 | async-start | bytes 3145728 | tf_op jit(solution)/shard_map/all_to_all | solution.py:79
  103.6 3.1 %collective-permute-start.1 = (bf16[4,1,256]{2,1,0:T(2,128)(2,1)S(1)}, bf16[4,1,256]{2,1,0:T(2,128)(2,1)S(1)}, u32[]{:S(2)}, u32[]{:S(2)}) collective-permute-start(bf16[4,1,256]{2,1,0:T(2,128)(2,1)S(1)} %get-tuple-element.16), channel_id=1, source_target_pairs={{16,0},{32,16},{48,32},{64,48},{80,64},{96,80},{112,96},{17,1},{33... | collective-permute-start | bytes 6152 | tf_op jit(solution)/shard_map/ppermute | solution.py:18
  106.7 2.4 collective-permute-start
  109.2 13.3 %collective-permute-done.1 = bf16[4,1,256]{2,1,0:T(2,128)(2,1)S(1)} collective-permute-done((bf16[4,1,256]{2,1,0:T(2,128)(2,1)S(1)}, bf16[4,1,256]{2,1,0:T(2,128)(2,1)S(1)}, u32[]{:S(2)}, u32[]{:S(2)}) %collective-permute-start.1) | collective-permute-done | bytes 2080 | tf_op jit(solution)/shard_map/ppermute | solution.py:18
  122.5 0.0 collective-permute-done
  122.5 0.1 pad_maximum_fusion
  122.5 0.1 fusion.20
  122.7 1.5 collective-permute-start.3
  124.1 4.0 %collective-permute-start.2 = (bf16[4,130,1]{2,1,0:T(8,128)(2,1)S(1)}, bf16[4,130,1]{2,1,0:T(8,128)(2,1)S(1)}, u32[]{:S(2)}, u32[]{:S(2)}) collective-permute-start(bf16[4,130,1]{2,1,0:T(8,128)(2,1)S(1)} %get-tuple-element.13), channel_id=1, source_target_pairs={{0,1},{1,2},{2,3},{3,4},{4,5},{5,6},{6,7},{7,8},{8,9},{9,10},{10,1... | collective-permute-start | bytes 3128 | tf_op jit(solution)/shard_map/ppermute | solution.py:17
  128.1 0.6 collective-permute-done.3
  128.8 1.4 collective-permute-done.2
  130.1 0.3 maximum_convert_fusion
  130.5 0.0 all-to-all-done.2
  130.5 0.1 broadcast_in_dim.36
  130.5 14.7 %scatter_fusion.1 = f32[128,4,256]{2,1,0:T(4,128)S(1)} fusion(f32[128,4,256]{2,1,0:T(4,128)S(1)} %broadcast_in_dim.36, s32[384]{0:T(512)S(1)} %reshape.126, f32[384,4,256]{2,1,0:T(4,128)S(1)} %bitcast.39), kind=kCustom, calls=%fused_computation.4 | custom fusion | flops 393216 | bytes 4720128 | tf_op jit(solution)/shard_map/scatter-add | solution.py:87
  145.2 0.1 copy.30
  145.3 2.6 reshape.90
  148.0 5.9 %copy.31 = f32[4,8,16,16,16]{4,3,2,1,0:T(8,128)} copy(f32[4,8,16,16,16]{4,2,3,1,0:T(8,128)} %bitcast.37) | data formatting | bytes 1048576 | tf_op jit(solution)/shard_map/transpose | solution.py:35
  153.8 0.0 copy-start
  153.8 0.0 copy-start.1
  153.8 3.6 %reshape.91 = f32[4,128,256]{2,1,0:T(8,128)S(1)} reshape(f32[4,8,16,16,16]{4,3,2,1,0:T(8,128)} %copy.31) | data formatting | bytes 1048576 | tf_op jit(solution)/shard_map/reshape | solution.py:36
  157.4 0.0 copy-done
  157.4 0.0 copy-done.1
  157.5 0.0 copy-start.3
  157.5 0.6 multiply_reduce_fusion.1
  158.0 72.0 %all-reduce = (f32[4]{0:T(128)S(1)}, f32[4]{0:T(128)S(1)}) all-reduce(f32[4]{0:T(128)S(1)} %get-tuple-element.17, f32[4]{0:T(128)S(1)} %get-tuple-element.7), channel_id=1, replica_groups=mesh['tx'=8,'ty'=16] {'tx','ty'}, use_global_device_ids=true, to_apply=%region_1.2 | all-reduce | flops 8 | bytes 64 | tf_op jit(solution)/shard_map/psum | solution.py:89
  230.1 0.2 multiply_reduce_fusion
  230.3 0.0 copy-start.2
  230.3 62.5 %psum.23 = f32[4]{0:T(128)S(1)} all-reduce(f32[4]{0:T(128)S(1)} %get-tuple-element.5), channel_id=1, replica_groups=mesh['tx'=8,'ty'=16] {'tx','ty'}, use_global_device_ids=true, to_apply=%region_11.12 | all-reduce | flops 4 | bytes 32 | tf_op jit(solution)/shard_map/psum | solution.py:93
  292.9 0.0 copy-done.3
  292.9 1.2 multiply_add_fusion
  294.0 0.0 copy-done.2
  (11 shorter events, 0.1 us)
Async XLA Ops:
  5.7 21.2 %all-to-all-start = ((s32[128,1,3]{2,1,0:T(1,128)}), s32[128,1,3]{2,1,0:T(1,128)S(1)}, u32[]{:S(2)}, u32[]{:S(2)}) async-start(s32[128,1,3]{2,1,0:T(1,128)} %bitcast.7), calls=%async_computation | async-start | bytes 131072 | tf_op jit(solution)/shard_map/all_to_all | solution.py:59
  31.4 24.7 %all-to-all-start.1 = ((bf16[128,3,4,256]{3,2,1,0:T(4,128)(2,1)}), bf16[128,3,4,256]{3,2,1,0:T(4,128)(2,1)S(1)}, u32[]{:S(2)}, u32[]{:S(2)}) async-start(bf16[128,3,4,256]{3,2,1,0:T(4,128)(2,1)} %broadcast_select_fusion), calls=%async_computation.1 | async-start | bytes 1572864 | tf_op jit(solution)/shard_map/all_to_all | solution.py:65
  99.4 31.1 %all-to-all-start.2 = ((f32[128,3,4,256]{3,2,1,0:T(4,128)}), f32[128,3,4,256]{3,2,1,0:T(4,128)S(1)}, u32[]{:S(2)}, u32[]{:S(2)}) async-start(f32[128,3,4,256]{3,2,1,0:T(4,128)} %bitcast.12), calls=%async_computation.2 | async-start | bytes 3145728 | tf_op jit(solution)/shard_map/all_to_all | solution.py:79
  103.6 18.9 %collective-permute-start.1 = (bf16[4,1,256]{2,1,0:T(2,128)(2,1)S(1)}, bf16[4,1,256]{2,1,0:T(2,128)(2,1)S(1)}, u32[]{:S(2)}, u32[]{:S(2)}) collective-permute-start(bf16[4,1,256]{2,1,0:T(2,128)(2,1)S(1)} %get-tuple-element.16), channel_id=1, source_target_pairs={{16,0},{32,16},{48,32},{64,48},{80,64},{96,80},{112,96},{17,1},{33... | collective-permute-start | bytes 6152 | tf_op jit(solution)/shard_map/ppermute | solution.py:18
  106.7 15.7 %collective-permute-start = (bf16[4,1,256]{2,1,0:T(2,128)(2,1)S(1)}, bf16[4,1,256]{2,1,0:T(2,128)(2,1)S(1)}, u32[]{:S(2)}, u32[]{:S(2)}) collective-permute-start(bf16[4,1,256]{2,1,0:T(2,128)(2,1)S(1)} %get-tuple-element.15), channel_id=1, source_target_pairs={{0,16},{16,32},{32,48},{48,64},{64,80},{80,96},{96,112},{1,17},{17... | collective-permute-start | bytes 6152 | tf_op jit(solution)/shard_map/ppermute | solution.py:17
  122.7 6.1 %collective-permute-start.3 = (bf16[4,130,1]{2,1,0:T(8,128)(2,1)S(1)}, bf16[4,130,1]{2,1,0:T(8,128)(2,1)S(1)}, u32[]{:S(2)}, u32[]{:S(2)}) collective-permute-start(bf16[4,130,1]{2,1,0:T(8,128)(2,1)S(1)} %get-tuple-element.14), channel_id=1, source_target_pairs={{1,0},{2,1},{3,2},{4,3},{5,4},{6,5},{7,6},{8,7},{9,8},{10,9},{11,1... | collective-permute-start | bytes 3128 | tf_op jit(solution)/shard_map/ppermute | solution.py:18
  124.1 6.0 %collective-permute-start.2 = (bf16[4,130,1]{2,1,0:T(8,128)(2,1)S(1)}, bf16[4,130,1]{2,1,0:T(8,128)(2,1)S(1)}, u32[]{:S(2)}, u32[]{:S(2)}) collective-permute-start(bf16[4,130,1]{2,1,0:T(8,128)(2,1)S(1)} %get-tuple-element.13), channel_id=1, source_target_pairs={{0,1},{1,2},{2,3},{3,4},{4,5},{5,6},{6,7},{7,8},{8,9},{9,10},{10,1... | collective-permute-start | bytes 3128 | tf_op jit(solution)/shard_map/ppermute | solution.py:17
  153.8 3.6 %copy-start = (f32[4,128,256]{2,1,0:T(8,128)S(1)}, f32[4,128,256]{2,1,0:T(8,128)}, u32[]{:S(2)}) copy-start(f32[4,128,256]{2,1,0:T(8,128)} %param.8) | copy-start | bytes 1572868
  153.8 3.6 %copy-start.1 = (f32[4,128,256]{2,1,0:T(8,128)S(1)}, f32[4,128,256]{2,1,0:T(8,128)}, u32[]{:S(2)}) copy-start(f32[4,128,256]{2,1,0:T(8,128)} %param.7) | copy-start | bytes 1572868
  157.5 135.4 %copy-start.3 = (f32[4,128,256]{2,1,0:T(8,128)S(1)}, f32[4,128,256]{2,1,0:T(8,128)}, u32[]{:S(2)}) copy-start(f32[4,128,256]{2,1,0:T(8,128)} %param.6) | copy-start | bytes 1572868
  230.3 63.7 %copy-start.2 = (f32[4,128,256]{2,1,0:T(8,128)}, f32[4,128,256]{2,1,0:T(8,128)S(1)}, u32[]{:S(2)}) copy-start(f32[4,128,256]{2,1,0:T(8,128)S(1)} %get-tuple-element.6) | copy-start | bytes 1572868
where the time goes:
time: 295 us; the launch traced here: 294 us
  blocking collectives  135 us (46%)
  local copies, waits for them, and re-layouts  51.6 us (17%)
  starting transfers between devices  34.7 us (12%)
  waiting for transfers between devices  33.7 us (11%)
  other arithmetic  21.7 us (7%)
  matrix products  16.9 us (6%)
    psum x1, blocking collectives, per_device(): norm_old = lax.psum(jnp.sum(residual * residual, axis=(1, 2)), ('tx', 'ty'))  72 us
    psum x1, blocking collectives, per_device(): lax.psum(jnp.sum(next_residual * next_residual, axis=(1, 2)), ('tx', 'ty'))  62.5 us
    scatter x1, local copies, waits for them, and re-layouts, per_device(): jnp.zeros((devices * cap, beacons, cells), jnp.float32).at[slot]  23.9 us
    dot_general x1, matrix products, per_device(): jnp.einsum('bsc,bks->bkc', blocks, samples, preferred_element_type=jnp.fl...  16.9 us
    all_to_all x1, waiting for transfers between devices, per_device(): lax.all_to_all(outgoing.reshape(devices, cap, beacons, cells), ('tx', 'ty...  16.6 us
    scatter-add x1, other arithmetic, per_device(): data_tiles = jnp.zeros(own_tiles.shape, jnp.float32).at[wanted].add(arrived)  14.7 us
    ppermute x2, waiting for transfers between devices, padded_2(): after = lax.ppermute(initial, axis, down)  13.9 us
    all_to_all x1, starting transfers between devices, per_device(): lax.all_to_all(request.reshape(devices, cap), ('tx', 'ty'), split_axis=0,...  11.5 us
  transfers between devices with their start and end apart: 7, of which 5 were waited for; matrix products, arithmetic and copies ran while one was open for 3% of the time, Pallas kernels for 0%

commit v1 on v0

--- a/solution.py
+++ b/solution.py
@@ -90,7 +90,7 @@
     curvature = lax.psum(jnp.sum(direction * image, axis=(1, 2)), ("tx", "ty"))
     alpha = norm_old / curvature
     next_residual = residual - alpha[:, None, None] * image
-    norm_new = lax.psum(jnp.sum(next_residual * next_residual, axis=(1, 2)), ("tx", "ty"))
+    norm_new = lax.psum(lax.psum(jnp.sum(next_residual * next_residual, axis=(1, 2)), "ty"), "tx")
     next_solution = solution + alpha[:, None, None] * direction
     next_direction = next_residual + (norm_new / norm_old)[:, None, None] * direction
     return (next_solution, next_residual, next_direction)

time: 295 us -> 283 us (0.959)
  blocking collectives: 135 us -> 123 us
    psum x1 -> x2, blocking collectives: 62.5 us -> 50.5 us  [the longest x1 30.8 us: per_device(): lax.psum(jnp.sum(next_residual * next_residual, axis=(1, 2)), 'ty')]
where the time goes in v1:
time: 283 us; the launch traced here: 282 us
  blocking collectives  123 us (43%)
  local copies, waits for them, and re-layouts  51.6 us (18%)
  starting transfers between devices  34.7 us (12%)
  waiting for transfers between devices  33.7 us (12%)
  other arithmetic  21.7 us (8%)
  matrix products  16.9 us (6%)
    psum x1, blocking collectives, per_device(): norm_old = lax.psum(jnp.sum(residual * residual, axis=(1, 2)), ('tx', 'ty'))  72 us
    psum x1, blocking collectives, per_device(): lax.psum(jnp.sum(next_residual * next_residual, axis=(1, 2)), 'ty')  30.8 us
    scatter x1, local copies, waits for them, and re-layouts, per_device(): jnp.zeros((devices * cap, beacons, cells), jnp.float32).at[slot]  23.9 us
    psum x1, blocking collectives, per_device(): lax.psum(lax.psum(jnp.sum(next_residual * next_residual, axis=(1, 2)), 't...  19.7 us
    dot_general x1, matrix products, per_device(): jnp.einsum('bsc,bks->bkc', blocks, samples, preferred_element_type=jnp.fl...  16.9 us
    all_to_all x1, waiting for transfers between devices, per_device(): lax.all_to_all(outgoing.reshape(devices, cap, beacons, cells), ('tx', 'ty...  16.6 us
    scatter-add x1, other arithmetic, per_device(): data_tiles = jnp.zeros(own_tiles.shape, jnp.float32).at[wanted].add(arrived)  14.7 us
    ppermute x2, waiting for transfers between devices, padded_2(): after = lax.ppermute(initial, axis, down)  13.9 us
  transfers between devices with their start and end apart: 7, of which 5 were waited for; matrix products, arithmetic and copies ran while one was open for 3% of the time, Pallas kernels for 0%

profile of v1, /device:TPU:1, one launch (start us, length us, event | category | flops | bytes accessed | tf_op | source)
XLA Modules:
  0.0 282.0 jit_solution(12175920984647356024)
XLA Ops:
  0.6 0.8 copy.23
  1.4 0.2 fusion.10
  1.7 0.9 fusion.12
  2.6 0.7 and_reduce_fusion
  3.3 1.6 scatter_custom_fusion
  4.8 0.8 all_to_all.12
  5.7 11.5 %all-to-all-start = ((s32[128,1,3]{2,1,0:T(1,128)}), s32[128,1,3]{2,1,0:T(1,128)S(1)}, u32[]{:S(2)}, u32[]{:S(2)}) async-start(s32[128,1,3]{2,1,0:T(1,128)} %bitcast.7), calls=%async_computation | async-start | bytes 131072 | tf_op jit(solution)/shard_map/all_to_all | solution.py:59
  17.2 1.1 convert_element_type.19
  18.3 2.5 reshape.85
  20.7 2.1 copy.33
  22.9 2.0 reshape.86
  24.9 0.2 copy.29
  25.1 1.8 all-to-all-done
  26.9 0.2 maximum_reduce_fusion
  27.1 0.2 reshape.126
  27.3 0.1 maximum_compare_fusion
  27.4 0.1 copy.26
  27.5 0.1 copy.27
  27.7 2.3 gather_fusion
  30.0 1.4 broadcast_select_fusion
  31.4 8.0 %all-to-all-start.1 = ((bf16[128,3,4,256]{3,2,1,0:T(4,128)(2,1)}), bf16[128,3,4,256]{3,2,1,0:T(4,128)(2,1)S(1)}, u32[]{:S(2)}, u32[]{:S(2)}) async-start(bf16[128,3,4,256]{3,2,1,0:T(4,128)(2,1)} %broadcast_select_fusion), calls=%async_computation.1 | async-start | bytes 1572864 | tf_op jit(solution)/shard_map/all_to_all | solution.py:65
  39.5 16.6 %all-to-all-done.1 = bf16[128,3,4,256]{3,2,1,0:T(4,128)(2,1)S(1)} async-done(((bf16[128,3,4,256]{3,2,1,0:T(4,128)(2,1)}), bf16[128,3,4,256]{3,2,1,0:T(4,128)(2,1)S(1)}, u32[]{:S(2)}, u32[]{:S(2)}) %all-to-all-start.1) | async-done | bytes 786464 | tf_op jit(solution)/shard_map/all_to_all | solution.py:65
  56.1 1.2 gather_fusion.1
  57.3 16.9 %fusion = f32[256,4,256]{2,1,0:T(4,128)S(1)} fusion(bf16[256,128,256]{2,1,0:T(8,128)(2,1)} %param.9, bf16[256,4,256]{2,1,0:T(4,128)(2,1)S(1)} %gather_fusion.1, pred[256]{0:T(512)(128)(4,1)S(1)} %get-tuple-element.9), kind=kOutput, calls=%fused_computation.8 | convolution fusion | flops 134610944 | bytes 18350336 | tf_op jit(solution)/shard_map/bsc,bks->bkc/dot_general | solution.py:77
  74.1 1.4 broadcast_in_dim.38
  75.5 23.9 %scatter_fusion = f32[384,4,256]{2,1,0:T(4,128)} fusion(f32[384,4,256]{2,1,0:T(4,128)} %broadcast_in_dim.38, s32[256]{0:T(256)S(1)} %bitcast.49, f32[256,4,256]{2,1,0:T(4,128)S(1)} %fusion), kind=kCustom, calls=%fused_computation.3 | custom fusion | bytes 3146752 | tf_op jit(solution)/shard_map/scatter | solution.py:78
  99.4 4.2 %all-to-all-start.2 = ((f32[128,3,4,256]{3,2,1,0:T(4,128)}), f32[128,3,4,256]{3,2,1,0:T(4,128)S(1)}, u32[]{:S(2)}, u32[]{:S(2)}) async-start(f32[128,3,4,256]{3,2,1,0:T(4,128)} %bitcast.12), calls=%async_computation.2 | async-start | bytes 3145728 | tf_op jit(solution)/shard_map/all_to_all | solution.py:79
  103.6 3.1 %collective-permute-start.1 = (bf16[4,1,256]{2,1,0:T(2,128)(2,1)S(1)}, bf16[4,1,256]{2,1,0:T(2,128)(2,1)S(1)}, u32[]{:S(2)}, u32[]{:S(2)}) collective-permute-start(bf16[4,1,256]{2,1,0:T(2,128)(2,1)S(1)} %get-tuple-element.16), channel_id=1, source_target_pairs={{16,0},{32,16},{48,32},{64,48},{80,64},{96,80},{112,96},{17,1},{33... | collective-permute-start | bytes 6152 | tf_op jit(solution)/shard_map/ppermute | solution.py:18
  106.7 2.4 collective-permute-start
  109.2 13.3 %collective-permute-done.1 = bf16[4,1,256]{2,1,0:T(2,128)(2,1)S(1)} collective-permute-done((bf16[4,1,256]{2,1,0:T(2,128)(2,1)S(1)}, bf16[4,1,256]{2,1,0:T(2,128)(2,1)S(1)}, u32[]{:S(2)}, u32[]{:S(2)}) %collective-permute-start.1) | collective-permute-done | bytes 2080 | tf_op jit(solution)/shard_map/ppermute | solution.py:18
  122.5 0.0 collective-permute-done
  122.5 0.1 pad_maximum_fusion
  122.5 0.1 fusion.20
  122.7 1.5 collective-permute-start.3
  124.1 4.0 %collective-permute-start.2 = (bf16[4,130,1]{2,1,0:T(8,128)(2,1)S(1)}, bf16[4,130,1]{2,1,0:T(8,128)(2,1)S(1)}, u32[]{:S(2)}, u32[]{:S(2)}) collective-permute-start(bf16[4,130,1]{2,1,0:T(8,128)(2,1)S(1)} %get-tuple-element.13), channel_id=1, source_target_pairs={{0,1},{1,2},{2,3},{3,4},{4,5},{5,6},{6,7},{7,8},{8,9},{9,10},{10,1... | collective-permute-start | bytes 3128 | tf_op jit(solution)/shard_map/ppermute | solution.py:17
  128.1 0.6 collective-permute-done.3
  128.8 1.4 collective-permute-done.2
  130.1 0.3 maximum_convert_fusion
  130.5 0.0 all-to-all-done.2
  130.5 0.1 broadcast_in_dim.36
  130.5 14.7 %scatter_fusion.1 = f32[128,4,256]{2,1,0:T(4,128)S(1)} fusion(f32[128,4,256]{2,1,0:T(4,128)S(1)} %broadcast_in_dim.36, s32[384]{0:T(512)S(1)} %reshape.126, f32[384,4,256]{2,1,0:T(4,128)S(1)} %bitcast.39), kind=kCustom, calls=%fused_computation.4 | custom fusion | flops 393216 | bytes 4720128 | tf_op jit(solution)/shard_map/scatter-add | solution.py:87
  145.2 0.1 copy.30
  145.3 2.6 reshape.90
  148.0 5.9 %copy.31 = f32[4,8,16,16,16]{4,3,2,1,0:T(8,128)} copy(f32[4,8,16,16,16]{4,2,3,1,0:T(8,128)} %bitcast.37) | data formatting | bytes 1048576 | tf_op jit(solution)/shard_map/transpose | solution.py:35
  153.8 0.0 copy-start
  153.8 0.0 copy-start.1
  153.8 3.6 %reshape.91 = f32[4,128,256]{2,1,0:T(8,128)S(1)} reshape(f32[4,8,16,16,16]{4,3,2,1,0:T(8,128)} %copy.31) | data formatting | bytes 1048576 | tf_op jit(solution)/shard_map/reshape | solution.py:36
  157.4 0.0 copy-done
  157.4 0.0 copy-done.1
  157.5 0.0 copy-start.3
  157.5 0.6 multiply_reduce_fusion.1
  158.0 72.0 %all-reduce = (f32[4]{0:T(128)S(1)}, f32[4]{0:T(128)S(1)}) all-reduce(f32[4]{0:T(128)S(1)} %get-tuple-element.17, f32[4]{0:T(128)S(1)} %get-tuple-element.7), channel_id=1, replica_groups=mesh['tx'=8,'ty'=16] {'tx','ty'}, use_global_device_ids=true, to_apply=%region_1.2 | all-reduce | flops 8 | bytes 64 | tf_op jit(solution)/shard_map/psum | solution.py:89
  230.1 0.2 multiply_reduce_fusion
  230.3 0.0 copy-start.2
  230.3 30.8 %psum.30 = f32[4]{0:T(128)S(1)} all-reduce(f32[4]{0:T(128)S(1)} %get-tuple-element.5), channel_id=1, replica_groups=mesh['tx'=8,'ty'=16] {'ty'}, use_global_device_ids=true, to_apply=%region_11.12 | all-reduce | flops 4 | bytes 32 | tf_op jit(solution)/shard_map/psum | solution.py:93
  261.1 19.7 %psum.31 = f32[4]{0:T(128)S(1)} all-reduce(f32[4]{0:T(128)S(1)} %psum.30), channel_id=1, replica_groups=mesh['tx'=8,'ty'=16] {'tx'}, use_global_device_ids=true, to_apply=%region_12.13 | all-reduce | flops 4 | bytes 32 | tf_op jit(solution)/shard_map/psum | solution.py:93
  280.8 0.0 copy-done.3
  280.8 1.2 multiply_add_fusion
  282.0 0.0 copy-done.2
  (11 shorter events, 0.1 us)
Async XLA Ops:
  5.7 21.2 %all-to-all-start = ((s32[128,1,3]{2,1,0:T(1,128)}), s32[128,1,3]{2,1,0:T(1,128)S(1)}, u32[]{:S(2)}, u32[]{:S(2)}) async-start(s32[128,1,3]{2,1,0:T(1,128)} %bitcast.7), calls=%async_computation | async-start | bytes 131072 | tf_op jit(solution)/shard_map/all_to_all | solution.py:59
  31.4 24.7 %all-to-all-start.1 = ((bf16[128,3,4,256]{3,2,1,0:T(4,128)(2,1)}), bf16[128,3,4,256]{3,2,1,0:T(4,128)(2,1)S(1)}, u32[]{:S(2)}, u32[]{:S(2)}) async-start(bf16[128,3,4,256]{3,2,1,0:T(4,128)(2,1)} %broadcast_select_fusion), calls=%async_computation.1 | async-start | bytes 1572864 | tf_op jit(solution)/shard_map/all_to_all | solution.py:65
  99.4 31.1 %all-to-all-start.2 = ((f32[128,3,4,256]{3,2,1,0:T(4,128)}), f32[128,3,4,256]{3,2,1,0:T(4,128)S(1)}, u32[]{:S(2)}, u32[]{:S(2)}) async-start(f32[128,3,4,256]{3,2,1,0:T(4,128)} %bitcast.12), calls=%async_computation.2 | async-start | bytes 3145728 | tf_op jit(solution)/shard_map/all_to_all | solution.py:79
  103.6 18.9 %collective-permute-start.1 = (bf16[4,1,256]{2,1,0:T(2,128)(2,1)S(1)}, bf16[4,1,256]{2,1,0:T(2,128)(2,1)S(1)}, u32[]{:S(2)}, u32[]{:S(2)}) collective-permute-start(bf16[4,1,256]{2,1,0:T(2,128)(2,1)S(1)} %get-tuple-element.16), channel_id=1, source_target_pairs={{16,0},{32,16},{48,32},{64,48},{80,64},{96,80},{112,96},{17,1},{33... | collective-permute-start | bytes 6152 | tf_op jit(solution)/shard_map/ppermute | solution.py:18
  106.7 15.7 %collective-permute-start = (bf16[4,1,256]{2,1,0:T(2,128)(2,1)S(1)}, bf16[4,1,256]{2,1,0:T(2,128)(2,1)S(1)}, u32[]{:S(2)}, u32[]{:S(2)}) collective-permute-start(bf16[4,1,256]{2,1,0:T(2,128)(2,1)S(1)} %get-tuple-element.15), channel_id=1, source_target_pairs={{0,16},{16,32},{32,48},{48,64},{64,80},{80,96},{96,112},{1,17},{17... | collective-permute-start | bytes 6152 | tf_op jit(solution)/shard_map/ppermute | solution.py:17
  122.7 6.1 %collective-permute-start.3 = (bf16[4,130,1]{2,1,0:T(8,128)(2,1)S(1)}, bf16[4,130,1]{2,1,0:T(8,128)(2,1)S(1)}, u32[]{:S(2)}, u32[]{:S(2)}) collective-permute-start(bf16[4,130,1]{2,1,0:T(8,128)(2,1)S(1)} %get-tuple-element.14), channel_id=1, source_target_pairs={{1,0},{2,1},{3,2},{4,3},{5,4},{6,5},{7,6},{8,7},{9,8},{10,9},{11,1... | collective-permute-start | bytes 3128 | tf_op jit(solution)/shard_map/ppermute | solution.py:18
  124.1 6.0 %collective-permute-start.2 = (bf16[4,130,1]{2,1,0:T(8,128)(2,1)S(1)}, bf16[4,130,1]{2,1,0:T(8,128)(2,1)S(1)}, u32[]{:S(2)}, u32[]{:S(2)}) collective-permute-start(bf16[4,130,1]{2,1,0:T(8,128)(2,1)S(1)} %get-tuple-element.13), channel_id=1, source_target_pairs={{0,1},{1,2},{2,3},{3,4},{4,5},{5,6},{6,7},{7,8},{8,9},{9,10},{10,1... | collective-permute-start | bytes 3128 | tf_op jit(solution)/shard_map/ppermute | solution.py:17
  153.8 3.6 %copy-start = (f32[4,128,256]{2,1,0:T(8,128)S(1)}, f32[4,128,256]{2,1,0:T(8,128)}, u32[]{:S(2)}) copy-start(f32[4,128,256]{2,1,0:T(8,128)} %param.8) | copy-start | bytes 1572868
  153.8 3.6 %copy-start.1 = (f32[4,128,256]{2,1,0:T(8,128)S(1)}, f32[4,128,256]{2,1,0:T(8,128)}, u32[]{:S(2)}) copy-start(f32[4,128,256]{2,1,0:T(8,128)} %param.7) | copy-start | bytes 1572868
  157.5 123.4 %copy-start.3 = (f32[4,128,256]{2,1,0:T(8,128)S(1)}, f32[4,128,256]{2,1,0:T(8,128)}, u32[]{:S(2)}) copy-start(f32[4,128,256]{2,1,0:T(8,128)} %param.6) | copy-start | bytes 1572868
  230.3 51.7 %copy-start.2 = (f32[4,128,256]{2,1,0:T(8,128)}, f32[4,128,256]{2,1,0:T(8,128)S(1)}, u32[]{:S(2)}) copy-start(f32[4,128,256]{2,1,0:T(8,128)S(1)} %get-tuple-element.6) | copy-start | bytes 1572868
